TPU v7x, 256 devices: a whole 4x4x8 slice. The times are simulated.
256 devices in a mesh: gy: 32 (over x, z_hi, core), gz: 8 (over z_lo, y).
Axes of the slice: x: 4, y: 4, z: 8 (z_hi: 4, z_lo: 2; z = z_hi * 2 + z_lo), core: 2. Of those that a mesh axis runs over, the one named last changes fastest.
Arguments:
- coeffs: bfloat16 [3, 512, 512, 512], P(None, 'gy', 'gz'), may hold values from -6 to 6
Outputs:
- current: float32 [3, 512, 512, 512], P(None, 'gy', 'gz')
- picture: float32 [4, 512, 512], P(None, 'gz', 'gy')
All inputs are finite; a program needn't handle non-finite values.
Results may differ from a plain program's by a relative error of at most 0.0051.
The roundings to bfloat16 on the way count: a program that leaves them out, or rounds other values in their place, can miss the bound.
Values may be sent and summed in bfloat16 or wider, within the bound.
A program may use at most 128 MiB of HBM per device.

v0:
```python
import math

import jax
import jax.numpy as jnp
from jax import lax
from jax.sharding import PartitionSpec as P

N = 512


def carried_in(shard, axis, join, neutral):
    place = lax.axis_index(axis)
    gathered = lax.all_gather(shard.astype(jnp.bfloat16), axis)
    state = jnp.zeros_like(shard) + jnp.asarray(neutral, shard.dtype)

    def one(lap, state):
        return join(state, lax.dynamic_index_in_dim(gathered, lap, 0, False).astype(shard.dtype))

    return lax.fori_loop(0, place, one, state)


def make_basis(length):
    mode_index = jnp.arange(length, dtype=jnp.int32)[:, None]
    cell_index = jnp.arange(length, dtype=jnp.int32)[None, :]
    half_size = length // 2
    frequency = jnp.where(mode_index <= half_size, mode_index, mode_index - half_size)
    phase_angle = (frequency * cell_index % length).astype(jnp.float32) * (2.0 * math.pi / length)
    values = jnp.where(
        mode_index <= half_size, jnp.cos(phase_angle), jnp.sin(phase_angle)
    ) * math.sqrt(2.0 / length)
    return values.astype(jnp.bfloat16)


def colormap(density):
    red_level = jnp.clip((density - 2.0) / 3.0, 0.0, 1.0)
    green_level = jnp.clip(1.0 - jnp.abs(density - 3.0) / 2.0, 0.0, 1.0)
    blue_level = jnp.clip(1.0 - density / 2.0, 0.0, 1.0)
    return 4.0 * jnp.stack([red_level, green_level, blue_level], axis=0)


def shards(coeffs):
    basis_table = make_basis(N)
    planes_x = coeffs.shape[1]
    modes_y = coeffs.shape[2]
    along_z = jnp.einsum(
        "cxmk,kz->cmzx", coeffs, basis_table, preferred_element_type=jnp.float32
    ).astype(jnp.bfloat16)
    along_z = along_z.reshape(3, modes_y, N * planes_x)
    along_y = jnp.einsum(
        "cmr,my->cyr",
        lax.all_to_all(along_z, "gz", split_axis=2, concat_axis=1, tiled=True),
        basis_table,
        preferred_element_type=jnp.float32,
    ).astype(jnp.bfloat16)
    received = lax.all_to_all(along_y, "gy", split_axis=1, concat_axis=2, tiled=True)
    senders = lax.axis_size("gy")
    shaped = received.reshape(received.shape[0], received.shape[1], senders, -1, planes_x)
    table_view = basis_table.reshape(senders, planes_x, N)
    current = jnp.einsum("cysql,sln->cyqn", shaped, table_view, preferred_element_type=jnp.float32)
    density = jnp.sum(current * current, axis=0)
    absorb = 0.6 / N
    optical = absorb * density
    before = jnp.cumsum(optical, axis=0) - optical
    weight = jnp.exp(-before) * (1.0 - jnp.exp(-optical))
    color_local = jnp.sum(weight[None] * colormap(density), axis=1)
    depth_sum = jnp.sum(optical, axis=0)

    def add_depths(earlier, later):
        return earlier + later

    depth_before = carried_in(depth_sum, "gy", add_depths, jnp.zeros_like(depth_sum))
    transmit = jnp.exp(-depth_before)
    terms = jnp.concatenate(
        [transmit[None] * color_local, (transmit * (1.0 - jnp.exp(-depth_sum)))[None]], axis=0
    )
    picture = lax.psum_scatter(terms, "gy", scatter_dimension=2, tiled=True)
    return (current, picture)


def solution(mesh):
    placed = (P(None, "gy", "gz", None),)
    return jax.shard_map(
        shards,
        mesh=mesh,
        in_specs=placed,
        out_specs=(P(None, "gy", "gz", None), P(None, "gz", "gy")),
        check_vma=False,
    )
```

profile of v0, /device:TPU:1, one launch (start us, length us, event | category | flops | bytes accessed | tf_op | source)
XLA Modules:
  0.0 648.2 jit_solution(2879379137695214437)
XLA Ops:
  7.2 1.9 copy-done
  9.1 9.0 %convert_bitcast_fusion.1 = bf16[3,64,512,16]{2,1,3,0:T(8,128)(2,1)} fusion(bf16[3,16,64,512]{3,2,1,0:T(8,128)(2,1)S(1)} %copy-done, s32[512]{0:T(512)S(1)} %add_select_fusion.3, pred[512]{0:T(512)(128)(4,1)S(1)} %iota_compare_fusion), kind=kOutput, calls=%fused_computation.5 | convolution fusion | flops 1616642048 | bytes 6294016 | tf_op jit(solution)/shard_map/cxmk,kz->cmzx/dot_general | solution.py:45
  18.1 8.5 %copy.24 = bf16[3,64,512,16]{1,3,2,0:T(8,128)(2,1)} copy(bf16[3,64,512,16]{2,1,3,0:T(8,128)(2,1)} %convert_bitcast_fusion.1) | data formatting | bytes 6291456 | tf_op jit(solution)/shard_map/convert_element_type | solution.py:47
  26.6 10.5 %copy.42 = bf16[3,64,8192]{1,0,2:T(4,128)(2,1)} copy(bf16[3,64,8192]{1,2,0:T(8,128)(2,1)} %bitcast.53) | data formatting | bytes 6291456 | tf_op jit(solution)/shard_map/reshape | solution.py:48
  37.1 8.6 %reshape.150 = bf16[8,2,98304]{2,1,0:T(2,128)(2,1)S(1)} reshape(bf16[8192,3,64]{2,1,0:T(4,128)(2,1)} %bitcast.51) | data formatting | bytes 6291456
  45.7 43.3 %all_to_all.33 = bf16[8,2,98304]{2,1,0:T(2,128)(2,1)} all-to-all(bf16[8,2,98304]{2,1,0:T(2,128)(2,1)S(1)} %reshape.150), channel_id=1, replica_groups=mesh['gy'=32,'gz'=8] {'gz'}, dimensions={0} | all-to-all | bytes 6291456 | tf_op jit(solution)/shard_map/all_to_all | solution.py:51
  89.0 9.5 %reshape.151 = bf16[8192,3,64]{2,1,0:T(4,128)(2,1)} reshape(bf16[8,2,98304]{2,1,0:T(2,128)(2,1)} %all_to_all.33) | data formatting | bytes 6291456
  98.5 12.2 %copy.39 = bf16[3,64,8,1024]{3,1,2,0:T(8,128)(2,1)} copy(bf16[3,64,8,1024]{1,0,3,2:T(4,128)(2,1)} %bitcast.52) | data formatting | bytes 6291456 | tf_op jit(solution)/shard_map/all_to_all | solution.py:51
  110.7 7.9 %convert_bitcast_fusion = bf16[3,512,1024]{2,1,0:T(8,128)(2,1)S(1)} fusion(bf16[3,512,1024]{2,1,0:T(8,128)(2,1)} %bitcast.54, s32[512]{0:T(512)S(1)} %add_select_fusion.3, pred[512]{0:T(512)(128)(4,1)S(1)} %iota_compare_fusion), kind=kOutput, calls=%fused_computation.4 | convolution fusion | flops 1616642048 | bytes 6294016 | tf_op jit(solution)/shard_map/cmr,my->cyr/dot_general | solution.py:49
  118.6 4.7 copy.28
  123.3 12.7 %all-to-all-start.1 = ((bf16[3,512,1024]{2,0,1:T(4,128)(2,1)}), bf16[3,512,1024]{2,0,1:T(4,128)(2,1)}, u32[]{:S(2)}, u32[]{:S(2)}) async-start(bf16[3,512,1024]{2,0,1:T(4,128)(2,1)} %copy.28), calls=%async_computation.1 | async-start | bytes 8388608 | tf_op jit(solution)/shard_map/all_to_all | solution.py:55
  136.1 95.9 %all-to-all-done.1 = bf16[3,512,1024]{2,0,1:T(4,128)(2,1)} async-done(((bf16[3,512,1024]{2,0,1:T(4,128)(2,1)}), bf16[3,512,1024]{2,0,1:T(4,128)(2,1)}, u32[]{:S(2)}, u32[]{:S(2)}) %all-to-all-start.1) | async-done | bytes 3145760 | tf_op jit(solution)/shard_map/all_to_all | solution.py:55
  232.0 13.8 %copy.29 = bf16[3,32,16,1024]{1,3,2,0:T(8,128)(2,1)} copy(bf16[3,32,16,1024]{3,0,2,1:T(4,128)(2,1)} %bitcast.10) | data formatting | bytes 6291456 | tf_op jit(solution)/shard_map/all_to_all | solution.py:55
  245.7 16.8 %copy.35 = bf16[3,16,32,64,16]{3,4,2,0,1:T(8,128)(2,1)} copy(bf16[3,16,32,64,16]{2,4,3,1,0:T(8,128)(2,1)} %bitcast.50) | data formatting | bytes 6291456 | tf_op jit(solution)/shard_map/reshape | solution.py:57
  262.6 10.8 %multiply_reduce_fusion = (f32[16,64,512]{2,1,0:T(8,128)S(1)}, f32[3,16,64,512]{3,2,0,1:T(8,128)}) fusion(bf16[3,16,32,64,16]{3,4,2,0,1:T(8,128)(2,1)} %copy.35, s32[32,16]{1,0:T(8,128)S(1)} %add_select_fusion.2, pred[32,16]{1,0:T(8,128)(4,1)S(1)} %fusion.29), kind=kOutput, calls=%fused_computation.3 | convolution fusion | flops 1617690624 | bytes 11536896 | tf_op jit(solution)/shard_map/cysql,sln->cyqn/dot_general | solution.py:59
  273.4 3.0 clamp_bitcast_fusion.2
  276.4 0.6 convert_element_type.55
  277.1 0.0 all-reduce.3.cloned.1.call-start
  277.2 0.9 multiply_multiply_fusion
  278.1 0.6 copy-done.2
  278.7 0.6 copy-done.3
  279.3 0.6 copy-done.4
  280.0 1.1 fusion
  281.1 47.4 %all-gather.3.cloned.1.call-done = bf16[2048,512]{1,0:T(8,128)(2,1)} async-done(((bf16[64,512]{1,0:T(8,128)(2,1)}), bf16[2048,512]{1,0:T(8,128)(2,1)}) %all-gather.3.cloned.1.call-update) | async-done | bytes 2097168 | tf_op jit(solution)/shard_map/all_gather | solution.py:13
  328.5 0.9 while.10
  328.5 0.9 convert_add_fusion.2
  329.5 1.3 copy.31
  330.9 0.6 dynamic-slice
  332.2 6.9 %copy.32 = f32[3,16,64,512]{3,2,1,0:T(8,128)} copy(f32[3,16,64,512]{3,2,0,1:T(8,128)} %get-tuple-element.49) | data formatting | bytes 12582912
  339.1 300.9 %all-reduce.3.cloned.1.call-done = f32[4,64,512]{1,0,2:T(4,128)} async-done(((f32[4,64,512]{1,0,2:T(4,128)}), f32[4,64,512]{1,0,2:T(4,128)}) %all-reduce.3.cloned.1.call-update) | async-done | bytes 524304
  640.0 0.8 constant_dynamic-slice_fusion
  640.8 0.6 copy.33
  (19 shorter events, 0.3 us)
Async XLA Ops:
  7.2 1.9 copy-start
  123.3 108.7 %all-to-all-start.1 = ((bf16[3,512,1024]{2,0,1:T(4,128)(2,1)}), bf16[3,512,1024]{2,0,1:T(4,128)(2,1)}, u32[]{:S(2)}, u32[]{:S(2)}) async-start(bf16[3,512,1024]{2,0,1:T(4,128)(2,1)} %copy.28), calls=%async_computation.1 | async-start | bytes 8388608 | tf_op jit(solution)/shard_map/all_to_all | solution.py:55
  136.0 192.4 %all-gather.3.cloned.1.call-start = ((), (), s32[]{:S(2)}) async-start(), calls=%async_computation.2 | async-start | bytes 2162688 | tf_op jit(solution)/shard_map/all_gather | solution.py:13
  277.1 362.9 %all-reduce.3.cloned.1.call-start = ((), (), s32[]{:S(2)}) async-start(), calls=%async_computation.3 | async-start | bytes 2097152
  277.1 1.6 copy-start.2
  277.1 2.2 copy-start.3
  277.1 2.8 copy-start.4
  329.4 1.5 copy-start.5
  332.2 309.2 %copy-start.1 = (bf16[3,16,64,512]{3,2,1,0:T(8,128)(2,1)S(1)}, bf16[3,16,64,512]{3,2,1,0:T(8,128)(2,1)}, u32[]{:S(2)}) copy-start(bf16[3,16,64,512]{3,2,1,0:T(8,128)(2,1)} %param.3) | copy-start | bytes 9437188
Sparse Core Ops, SparseCore 0:
  277.2 51.2 all-gather.2
  331.1 308.8 all-reduce.2
where the time goes:
time: 651 us; the launch traced here: 648 us
  waiting for transfers between devices  444 us (68%)
  local copies, waits for them, and re-layouts  98.6 us (15%)
  blocking collectives  43.3 us (7%)
  matrix products  27.7 us (4%)
  between operations  14.9 us (2%)
  starting transfers between devices  12.8 us (2%)
  other arithmetic  6.63 us (1%)
    unnamed x3, waiting for transfers between devices  301 us
    all_to_all x1, waiting for transfers between devices, shards(): lax.all_to_all(along_y, 'gy', split_axis=1, concat_axis=2, tiled=True)  95.9 us
    all_gather x1, waiting for transfers between devices, carried_in(): gathered = lax.all_gather(shard.astype(jnp.bfloat16), axis)  47.4 us
    all_to_all x1, blocking collectives, shards(): lax.all_to_all(along_z, 'gz', split_axis=2, concat_axis=1, tiled=True)  43.3 us
    unnamed x18, local copies, waits for them, and re-layouts  30.8 us
    reshape x1, local copies, waits for them, and re-layouts, shards(): received.reshape(received.shape[0], received.shape[1], senders, -1, plane...  16.8 us
    all_to_all x1, local copies, waits for them, and re-layouts, shards(): lax.all_to_all(along_y, 'gy', split_axis=1, concat_axis=2, tiled=True)  13.8 us
  transfers between devices with their start and end apart: 3, of which 3 were waited for; matrix products, arithmetic and copies ran while one was open for 1% of the time, Pallas kernels for 0%

commit v1 on v0

v1 whole, which is shorter than its diff:
```python
import functools
import math

import jax
import jax.numpy as jnp
import ml_dtypes
import numpy as np
from jax import lax
from jax.experimental import pallas as pl
from jax.experimental.pallas import tpu as pltpu
from jax.sharding import PartitionSpec as P

N = 512
J = 4
ZC = 16
MESH = pl.DeviceIdType.MESH
BF, F32 = jnp.bfloat16, jnp.float32


def make_basis(length):
    mode_index = np.arange(length, dtype=np.int32)[:, None]
    cell_index = np.arange(length, dtype=np.int32)[None, :]
    half_size = length // 2
    frequency = np.where(mode_index <= half_size, mode_index, mode_index - half_size)
    phase_angle = (frequency * cell_index % length).astype(np.float32) * np.float32(2.0 * math.pi / length)
    values = np.where(mode_index <= half_size, np.cos(phase_angle), np.sin(phase_angle)) * np.float32(
        math.sqrt(2.0 / length)
    )
    return values.astype(ml_dtypes.bfloat16)


def tables():
    basis = make_basis(N)
    order_z = np.arange(N).reshape(8, J, ZC).transpose(1, 0, 2).reshape(-1)
    table_z = np.ascontiguousarray(basis.T[order_z])
    table_y = np.zeros((2, N, 8, 2, 64), ml_dtypes.bfloat16)
    for parity in range(2):
        table_y[parity, :, :, parity, :] = basis.T.reshape(N, 8, 64)
    table_y = table_y.reshape(2 * N, 2 * N)
    group, pair, tile = np.meshgrid(np.arange(4), np.arange(8), np.arange(16), indexing="ij")
    slot = group * 16 + tile
    order_x = ((slot // 2) * 16 + pair * 2 + slot % 2).reshape(-1)
    table_x = np.ascontiguousarray(basis[order_x])
    return table_z, table_y, table_x


def kernel(
    coef_hbm, tz_hbm, ty_hbm, tx_hbm, current_hbm, bricks_ref,
    coef, tz, ty, tx, sent1, got1, sent2, got2, rows_x, field, tint, pic_out, pic_in,
    load_sem, send1, recv1, send2, recv2, send3, recv3, store_sem,
):
    gy, gz = lax.axis_index("gy"), lax.axis_index("gz")

    def gy_at(step):
        gx = lax.rem(gy // 8 + step // 8, 4)
        gh = lax.rem(lax.rem(gy // 2, 4) + lax.rem(step // 2, 4), 4)
        gc = lax.rem(gy + step, 2)
        return gx * 8 + gh * 2 + gc

    def gz_at(step):
        return lax.rem(gz // 4 + step // 4, 2) * 4 + lax.rem(gz + step, 4)

    barrier = pltpu.get_barrier_semaphore()

    def greet_z(step, carry):
        pl.semaphore_signal(barrier, inc=1, device_id=(gy, gz_at(step)), device_id_type=MESH)
        return carry

    def greet_y(step, carry):
        pl.semaphore_signal(barrier, inc=1, device_id=(gy_at(step), gz), device_id_type=MESH)
        return carry

    loads = [
        pltpu.make_async_copy(tz_hbm, tz, load_sem.at[0]),
        pltpu.make_async_copy(coef_hbm, coef, load_sem.at[1]),
        pltpu.make_async_copy(ty_hbm, ty, load_sem.at[2]),
        pltpu.make_async_copy(tx_hbm, tx, load_sem.at[3]),
    ]
    for load in loads:
        load.start()
    lax.fori_loop(1, 8, greet_z, 0)
    lax.fori_loop(1, 32, greet_y, 0)
    loads[0].wait()
    loads[1].wait()

    def transform_z(chunk):
        def one(p, carry):
            out = lax.dot_general(
                tz[pl.ds(chunk * 128, 128), :], coef[p], (((1,), (1,)), ((), ())), preferred_element_type=F32
            ).astype(BF)
            for q in range(8):
                sent1[chunk, q, p] = out[q * ZC : (q + 1) * ZC]
            return carry

        lax.fori_loop(0, 24, one, 0, unroll=4)

    def send_z(chunk):
        pltpu.make_async_copy(sent1.at[chunk, gz], got1.at[chunk, gz], recv1.at[chunk]).start()

        def one(step, carry):
            to = gz_at(step)
            pltpu.make_async_remote_copy(
                src_ref=sent1.at[chunk, to], dst_ref=got1.at[chunk, gz],
                send_sem=send1.at[chunk], recv_sem=recv1.at[chunk],
                device_id=(gy, to), device_id_type=MESH,
            ).start()
            return carry

        lax.fori_loop(1, 8, one, 0)

    transform_z(0)
    pl.semaphore_wait(barrier, 38)

    def stage_z(chunk, carry):
        send_z(chunk)

        @pl.when(chunk < J - 1)
        def _():
            transform_z(chunk + 1)

        return carry

    lax.fori_loop(0, J, stage_z, 0)
    loads[2].wait()
    loads[3].wait()

    def stage_y(chunk, carry):
        pltpu.make_async_copy(got1.at[chunk], got1.at[chunk], recv1.at[chunk]).wait()

        def one(c, inner):
            rows = jnp.concatenate(
                [got1[chunk, s, pl.ds(c * 8, 8)].reshape(128, 128) for s in range(8)], axis=1
            )
            for half in range(2):
                out = lax.dot_general(
                    ty[half * N : (half + 1) * N, :], rows, (((1,), (1,)), ((), ())), preferred_element_type=F32
                ).astype(BF)
                for g in range(32):
                    sent2[chunk, g, c, half] = out[g * 16 : (g + 1) * 16]
            return inner

        lax.fori_loop(0, 3, one, 0)
        pltpu.make_async_copy(sent2.at[chunk, gy], got2.at[chunk, gy], recv2.at[chunk]).start()

        def push(step, inner):
            to = gy_at(step)
            pltpu.make_async_remote_copy(
                src_ref=sent2.at[chunk, to], dst_ref=got2.at[chunk, gy],
                send_sem=send2.at[chunk], recv_sem=recv2.at[chunk],
                device_id=(to, gz), device_id_type=MESH,
            ).start()
            return inner

        lax.fori_loop(1, 32, push, 0)
        return carry

    lax.fori_loop(0, J, stage_y, 0)

    lane = lax.broadcasted_iota(jnp.int32, (16, 128), 1)

    def stage_x(chunk, carry):
        pltpu.make_async_copy(got2.at[chunk], got2.at[chunk], recv2.at[chunk]).wait()

        def component(c, inner):
            for group in range(4):
                tiles = [got2[chunk, group * 8 + t // 2, c, t % 2].astype(F32) for t in range(16)]
                for bit in (1, 2, 4, 8):
                    low = (lane & bit) == 0
                    for t in range(16):
                        if t & bit == 0:
                            u, v = tiles[t], tiles[t + bit]
                            tiles[t] = jnp.where(low, u, pltpu.roll(v, bit, 1))
                            tiles[t + bit] = jnp.where(low, pltpu.roll(u, 128 - bit, 1), v)
                for t in range(16):
                    rows_x[pl.ds(t * 16, 16), pl.ds(group * 128, 128)] = tiles[t].astype(BF)
            out = jnp.dot(rows_x[...], tx[...], preferred_element_type=F32)
            for col in range(4):
                for t in range(16):
                    field[chunk, c, col, pl.ds(t, 16, stride=ZC), :] = out[
                        t * 16 : (t + 1) * 16, col * 128 : (col + 1) * 128
                    ]
                pltpu.make_async_copy(
                    field.at[chunk, c, col].reshape(16, ZC, 128),
                    current_hbm.at[c, :, pl.ds(chunk * ZC, ZC), pl.ds(col * 128, 128)],
                    store_sem.at[chunk, c],
                ).start()
            return inner

        lax.fori_loop(0, 3, component, 0)
        absorb = 0.6 / N
        for col in range(4):
            cols = pl.ds(col * 128, 128)
            passed = jnp.ones((ZC, 128), F32)
            depth = jnp.zeros((ZC, 128), F32)
            colors = [jnp.zeros((ZC, 128), F32)] * 3
            for y in range(16):
                parts = [field[chunk, c, col, pl.ds(y * ZC, ZC), :] for c in range(3)]
                density = parts[0] * parts[0] + parts[1] * parts[1] + parts[2] * parts[2]
                optical = absorb * density
                left = jnp.exp(-optical)
                weight = 4.0 * (passed * (1.0 - left))
                passed = passed * left
                depth = depth + optical
                levels = (
                    jnp.clip((density - 2.0) * (1.0 / 3.0), 0.0, 1.0),
                    jnp.clip(1.0 - jnp.abs(density - 3.0) * 0.5, 0.0, 1.0),
                    jnp.clip(1.0 - density * 0.5, 0.0, 1.0),
                )
                colors = [color + weight * level for color, level in zip(colors, levels)]
            part = lax.rem(chunk, 2)
            for k, value in enumerate(colors + [depth]):
                tint[pl.ds(part * 64 + k * ZC, ZC), cols] = value

        @pl.when(lax.rem(chunk, 2) == 1)
        def _():
            pair = chunk // 2
            for col in range(4):
                turned = jnp.transpose(tint[:, col * 128 : (col + 1) * 128]).astype(BF)
                for g in range(8):
                    pic_out[pair, col * 8 + g] = turned[g * 16 : (g + 1) * 16]
            pltpu.make_async_copy(pic_out.at[pair, gy], pic_in.at[pair, gy], recv3.at[pair]).start()

            def push(step, inner):
                to = gy_at(step)
                pltpu.make_async_remote_copy(
                    src_ref=pic_out.at[pair, to], dst_ref=pic_in.at[pair, gy],
                    send_sem=send3.at[pair], recv_sem=recv3.at[pair],
                    device_id=(to, gz), device_id_type=MESH,
                ).start()
                return inner

            lax.fori_loop(1, 32, push, 0)

        return carry

    lax.fori_loop(0, J, stage_x, 0)

    channel = (lane // ZC) % 4
    is_depth = channel == 3

    def combine(pair, carry):
        pltpu.make_async_copy(pic_in.at[pair], pic_in.at[pair], recv3.at[pair]).wait()
        before = jnp.zeros((16, 128), F32)
        total = jnp.zeros((16, 128), F32)
        for s in range(32):
            brick = pic_in[pair, s].astype(F32)
            depth = jnp.where(is_depth, brick, 0.0)
            depth = depth + pltpu.roll(depth, 128 - 16, 1)
            depth = depth + pltpu.roll(depth, 128 - 32, 1)
            total = total + jnp.exp(-before) * brick
            before = before + depth
        bricks_ref[pair] = jnp.where(is_depth, 1.0 - jnp.exp(-before), total)
        return carry

    lax.fori_loop(0, 2, combine, 0)

    for chunk in range(J):
        first = sent1.at[chunk, pl.ds(0, 7)]
        pltpu.make_async_copy(first, first, send1.at[chunk]).wait()
        second = sent2.at[chunk, pl.ds(0, 31)]
        pltpu.make_async_copy(second, second, send2.at[chunk]).wait()
        for c in range(3):
            pltpu.make_async_copy(field.at[chunk, c], field.at[chunk, c], store_sem.at[chunk, c]).wait()
    for pair in range(2):
        third = pic_out.at[pair, pl.ds(0, 31)]
        pltpu.make_async_copy(third, third, send3.at[pair]).wait()


def shards(coeffs):
    table_z, table_y, table_x = (jnp.asarray(table) for table in tables())
    any_space = pl.BlockSpec(memory_space=pl.ANY)
    current, bricks = pl.pallas_call(
        kernel,
        out_shape=(
            jax.ShapeDtypeStruct((3, 16, 64, N), F32),
            jax.ShapeDtypeStruct((2, 16, 128), F32),
        ),
        in_specs=[any_space] * 4,
        out_specs=(any_space, pl.BlockSpec(memory_space=pltpu.VMEM)),
        scratch_shapes=[
            pltpu.VMEM((24, 128, N), BF),
            pltpu.VMEM((N, N), BF),
            pltpu.VMEM((2 * N, 2 * N), BF),
            pltpu.VMEM((N, N), BF),
            pltpu.VMEM((J, 8, 24, ZC, 128), BF),
            pltpu.VMEM((J, 8, 24, ZC, 128), BF),
            pltpu.VMEM((J, 32, 3, 2, 16, 128), BF),
            pltpu.VMEM((J, 32, 3, 2, 16, 128), BF),
            pltpu.VMEM((256, N), BF),
            pltpu.VMEM((J, 3, 4, 16 * ZC, 128), F32),
            pltpu.VMEM((128, N), F32),
            pltpu.VMEM((2, 32, 16, 128), BF),
            pltpu.VMEM((2, 32, 16, 128), BF),
            pltpu.SemaphoreType.DMA((4,)),
            pltpu.SemaphoreType.DMA((J,)),
            pltpu.SemaphoreType.DMA((J,)),
            pltpu.SemaphoreType.DMA((J,)),
            pltpu.SemaphoreType.DMA((J,)),
            pltpu.SemaphoreType.DMA((2,)),
            pltpu.SemaphoreType.DMA((2,)),
            pltpu.SemaphoreType.DMA((J, 3)),
        ],
        compiler_params=pltpu.CompilerParams(
            collective_id=0, has_side_effects=True, vmem_limit_bytes=48 * 1024 * 1024
        ),
        name="render",
    )(coeffs.reshape(24, 128, N), table_z, table_y, table_x)
    picture = bricks.reshape(2, 16, 2, 4, ZC).transpose(3, 0, 2, 4, 1).reshape(4, 64, 16)
    return (current, picture)


def solution(mesh):
    return jax.shard_map(
        shards,
        mesh=mesh,
        in_specs=(P(None, "gy", "gz", None),),
        out_specs=(P(None, "gy", "gz", None), P(None, "gz", "gy")),
        check_vma=False,
    )
```

time: 651 us -> 143 us (0.22)
  waiting for transfers between devices: 444 us -> 0 us
  Pallas kernels: 0 us -> 131 us
  local copies, waits for them, and re-layouts: 98.6 us -> 11.4 us
  blocking collectives: 43.3 us -> 0 us
  matrix products: 27.7 us -> 0 us
  between operations: 14.9 us -> 0.66 us
  starting transfers between devices: 12.8 us -> 0 us
  other arithmetic: 6.63 us -> 0 us
    unnamed x3 -> x0, waiting for transfers between devices: 301 us -> none
    pallas_call x0 -> x1, Pallas kernels: none -> 131 us  [shards(): pl.pallas_call(kernel, out_shape=(jax.ShapeDtypeStruct((3, 16, 64, N), F3...]
    all_to_all x1 -> x0, waiting for transfers between devices: 95.9 us -> none  [shards(): lax.all_to_all(along_y, 'gy', split_axis=1, concat_axis=2, tiled=True)]
    all_gather x1 -> x0, waiting for transfers between devices: 47.4 us -> none  [carried_in(): gathered = lax.all_gather(shard.astype(jnp.bfloat16), axis)]
    all_to_all x1 -> x0, blocking collectives: 43.3 us -> none  [shards(): lax.all_to_all(along_z, 'gz', split_axis=2, concat_axis=1, tiled=True)]
    dot_general x3 -> x0, matrix products: 27.7 us -> none  [the longest x1 10.8 us: shards(): jnp.einsum('cysql,sln->cyqn', shaped, table_view, preferred_element_type=...]
    reshape x2, local copies, waits for them, and re-layouts: 27.3 us -> 0.9 us  [shards(): bricks.reshape(2, 16, 2, 4, ZC).transpose(3, 0, 2, 4, 1).reshape(4, 64, 16)]
    all_to_all x2 -> x0, local copies, waits for them, and re-layouts: 26 us -> none  [the longest x1 13.8 us: shards(): lax.all_to_all(along_y, 'gy', split_axis=1, concat_axis=2, tiled=True)]
  transfers between devices with their start and end apart: 3 -> 0, of which waited for: 3 -> 0; matrix products, arithmetic and copies ran while one was open for 1% -> 0% of each run, Pallas kernels for 0% -> 0%
where the time goes in v1:
time: 143 us
  Pallas kernels  131 us (92%)
  local copies, waits for them, and re-layouts  11.4 us (8%)
    pallas_call x1, Pallas kernels, shards(): pl.pallas_call(kernel, out_shape=(jax.ShapeDtypeStruct((3, 16, 64, N), F3...  131 us
    unnamed x7, local copies, waits for them, and re-layouts  10.4 us

profile of v1, /device:TPU:1, one launch (start us, length us, event | category | flops | bytes accessed | tf_op | source)
XLA Modules:
  0.0 142.9 jit_solution(1914705926225503269)
XLA Ops:
  0.6 0.0 copy-start
  0.6 1.6 %copy-done = bf16[1024,1024]{1,0:T(8,128)(2,1)S(1)} copy-done((bf16[1024,1024]{1,0:T(8,128)(2,1)S(1)}, bf16[1024,1024]{1,0:T(8,128)(2,1)}, u32[]{:S(2)}) %copy-start) | copy-done | bytes 2097176
  2.2 0.0 copy-start.1
  2.2 1.0 copy-done.1
  3.3 0.0 copy-start.2
  3.3 1.0 copy-done.2
  4.3 130.8 %render.1 = (f32[3,16,64,512]{3,2,1,0:T(8,128)}, f32[2,16,128]{2,1,0:T(8,128)S(1)}) custom-call(bf16[24,128,512]{2,1,0:T(8,128)(2,1)} %bitcast.4, bf16[512,512]{1,0:T(8,128)(2,1)S(1)} %copy-done.2, bf16[1024,1024]{1,0:T(8,128)(2,1)S(1)} %copy-done, bf16[512,512]{1,0:T(8,128)(2,1)S(1)} %copy-done.1), custom_call_target="tpu_custom_call" | custom-call | tf_op jit(solution)/shard_map/render/pallas_call | solution.py:272
  135.2 0.1 reshape.14
  135.3 0.1 copy.6
  135.4 0.8 reshape.15
  136.1 6.7 %copy.8 = f32[3,16,64,512]{3,2,1,0:T(8,128)} copy(f32[3,16,64,512]{3,2,1,0:T(8,128)} %get-tuple-element.8) | data formatting | bytes 12582912
Async XLA Ops:
  0.6 1.6 %copy-start = (bf16[1024,1024]{1,0:T(8,128)(2,1)S(1)}, bf16[1024,1024]{1,0:T(8,128)(2,1)}, u32[]{:S(2)}) copy-start(bf16[1024,1024]{1,0:T(8,128)(2,1)} %constant.7.clone.ty_hbm) | copy-start | bytes 6291460
  2.2 1.0 copy-start.1
  3.3 1.0 copy-start.2

commit v2 on v1

--- a/solution.py
+++ b/solution.py
@@ -29,132 +29,234 @@
     return values.astype(ml_dtypes.bfloat16)
 
 
+SLOTS = 136
+PAIRS = ((0, 3), (1, 2))
+
+
+def cells_of(half):
+    blocks = [x * 8 + hi * 2 + core for x in range(4) for hi in PAIRS[half] for core in range(2)]
+    return np.array([block * 16 + i for block in blocks for i in range(16)])
+
+
+def slots_of(z_lo, half):
+    cells = cells_of(half)
+    folded = sorted(set(np.minimum(cells, N - cells).tolist()))
+    if z_lo == 1:
+        folded = [cell for cell in folded if cell not in (0, N // 2)]
+    return folded
+
+
 def tables():
-    basis = make_basis(N)
-    order_z = np.arange(N).reshape(8, J, ZC).transpose(1, 0, 2).reshape(-1)
+    basis = make_basis(N).astype(np.float32)
+    order_z = np.arange(N).reshape(2, 4, J, ZC).transpose(2, 1, 0, 3).reshape(-1)
     table_z = np.ascontiguousarray(basis.T[order_z])
-    table_y = np.zeros((2, N, 8, 2, 64), ml_dtypes.bfloat16)
-    for parity in range(2):
-        table_y[parity, :, :, parity, :] = basis.T.reshape(N, 8, 64)
-    table_y = table_y.reshape(2 * N, 2 * N)
+    keep = np.zeros((4, 2, 256, 4, 2, 64), np.float32)
+    give = np.zeros((4, 2, SLOTS, 4, 2, 64), np.float32)
+    take = np.zeros((4, 2, 256, 2, SLOTS), np.float32)
+    for z_lo in range(2):
+        modes = slice(z_lo * 256, z_lo * 256 + 256)
+        for half in range(2):
+            kind = z_lo * 2 + half
+            cells = cells_of(half)
+            own = basis[modes, :][:, cells].T.reshape(256, 4, 64)
+            slots = slots_of(z_lo, 1 - half)
+            sums = np.zeros((SLOTS, 256), np.float32)
+            sums[: len(slots)] = basis[modes, :][:, slots].T
+            if z_lo == 1:
+                sums[:, 0] = 0.0
+                sums[len(slots), 0] = basis[256, 0]
+            unfold = np.zeros((256, SLOTS), np.float32)
+            theirs = slots_of(1 - z_lo, half)
+            for row, cell in enumerate(cells):
+                folded = min(cell, N - cell)
+                if folded in theirs:
+                    unfold[row, theirs.index(folded)] = 1.0 if z_lo == 1 or cell < N // 2 else -1.0
+                if z_lo == 0:
+                    unfold[row, len(theirs)] = 1.0 - 2.0 * (cell % 2)
+            for parity in range(2):
+                keep[kind, parity, :, :, parity] = own
+                give[kind, parity, :, :, parity] = sums.reshape(SLOTS, 4, 64)
+                take[kind, parity, :, parity] = unfold
     group, pair, tile = np.meshgrid(np.arange(4), np.arange(8), np.arange(16), indexing="ij")
     slot = group * 16 + tile
     order_x = ((slot // 2) * 16 + pair * 2 + slot % 2).reshape(-1)
     table_x = np.ascontiguousarray(basis[order_x])
-    return table_z, table_y, table_x
+    return (
+        table_z,
+        np.concatenate([keep.reshape(4, 512, 512), give.reshape(4, 2 * SLOTS, 512)], axis=1),
+        take.reshape(4, 512, 2 * SLOTS),
+        table_x,
+    )
 
 
 def kernel(
-    coef_hbm, tz_hbm, ty_hbm, tx_hbm, current_hbm, bricks_ref,
-    coef, tz, ty, tx, sent1, got1, sent2, got2, rows_x, field, tint, pic_out, pic_in,
-    load_sem, send1, recv1, send2, recv2, send3, recv3, store_sem,
+    coef_hbm, tz_hbm, ty_hbm, take_hbm, tx_hbm, current_hbm, bricks_ref,
+    raw_z, raw_y, raw_take, raw_x,
+    coef, tz, ty, take, tx, sent1, got1, half_out, half_in, sent2, got2, rows_x, field, tint, pic_out, pic_in,
+    load_sem, send1, recv1, sendh, recvh, send2, recv2, send3, recv3, store_sem,
 ):
     gy, gz = lax.axis_index("gy"), lax.axis_index("gz")
+    at_x, at_hi, at_core = gy // 8, lax.rem(gy // 2, 4), lax.rem(gy, 2)
+    at_lo, at_y = gz // 4, lax.rem(gz, 4)
+    half = lax.rem(at_lo + at_hi // 2, 2)
+    kind = at_lo * 2 + half
+    in_half = half == lax.rem((at_hi + 1) // 2, 2)
 
     def gy_at(step):
-        gx = lax.rem(gy // 8 + step // 8, 4)
-        gh = lax.rem(lax.rem(gy // 2, 4) + lax.rem(step // 2, 4), 4)
-        gc = lax.rem(gy + step, 2)
+        gx = lax.rem(at_x + step // 8, 4)
+        gh = lax.rem(at_hi + lax.rem(step // 2, 4), 4)
+        gc = lax.rem(at_core + step, 2)
         return gx * 8 + gh * 2 + gc
 
-    def gz_at(step):
-        return lax.rem(gz // 4 + step // 4, 2) * 4 + lax.rem(gz + step, 4)
+    def y_at(step):
+        return at_lo * 4 + lax.rem(at_y + step, 4)
+
+    twin = (1 - at_lo) * 4 + at_y
 
     barrier = pltpu.get_barrier_semaphore()
 
-    def greet_z(step, carry):
-        pl.semaphore_signal(barrier, inc=1, device_id=(gy, gz_at(step)), device_id_type=MESH)
+    def greet(step, carry):
+        to = gy_at(step)
+        pl.semaphore_signal(barrier, inc=1, device_id=(to, gz), device_id_type=MESH)
+        pl.semaphore_signal(barrier, inc=1, device_id=(to, twin), device_id_type=MESH)
         return carry
 
-    def greet_y(step, carry):
-        pl.semaphore_signal(barrier, inc=1, device_id=(gy_at(step), gz), device_id_type=MESH)
-        return carry
-
     loads = [
-        pltpu.make_async_copy(tz_hbm, tz, load_sem.at[0]),
+        pltpu.make_async_copy(tz_hbm, raw_z, load_sem.at[0]),
         pltpu.make_async_copy(coef_hbm, coef, load_sem.at[1]),
-        pltpu.make_async_copy(ty_hbm, ty, load_sem.at[2]),
-        pltpu.make_async_copy(tx_hbm, tx, load_sem.at[3]),
+        pltpu.make_async_copy(ty_hbm.at[kind], raw_y, load_sem.at[2]),
+        pltpu.make_async_copy(take_hbm.at[kind], raw_take, load_sem.at[3]),
+        pltpu.make_async_copy(tx_hbm, raw_x, load_sem.at[4]),
     ]
     for load in loads:
         load.start()
-    lax.fori_loop(1, 8, greet_z, 0)
-    lax.fori_loop(1, 32, greet_y, 0)
+    for step in range(1, 4):
+        pl.semaphore_signal(barrier, inc=1, device_id=(gy, y_at(step)), device_id_type=MESH)
+    pl.semaphore_signal(barrier, inc=1, device_id=(gy, twin), device_id_type=MESH)
+    lax.fori_loop(1, 32, greet, 0)
     loads[0].wait()
+    tz[...] = raw_z[...].astype(BF)
     loads[1].wait()
 
-    def transform_z(chunk):
+    def transform_z(unit):
+        chunk, c = unit // 3, lax.rem(unit, 3)
+
         def one(p, carry):
             out = lax.dot_general(
-                tz[pl.ds(chunk * 128, 128), :], coef[p], (((1,), (1,)), ((), ())), preferred_element_type=F32
+                tz[pl.ds(pl.multiple_of(chunk * 128, 128), 128), :], coef[c * 8 + p], (((1,), (1,)), ((), ())),
+                preferred_element_type=F32,
             ).astype(BF)
-            for q in range(8):
-                sent1[chunk, q, p] = out[q * ZC : (q + 1) * ZC]
+            for y in range(4):
+                for lo in range(2):
+                    row = (y * 2 + lo) * ZC
+                    sent1[chunk, c, y, lo, p] = out[row : row + ZC]
             return carry
 
-        lax.fori_loop(0, 24, one, 0, unroll=4)
-
-    def send_z(chunk):
-        pltpu.make_async_copy(sent1.at[chunk, gz], got1.at[chunk, gz], recv1.at[chunk]).start()
-
-        def one(step, carry):
-            to = gz_at(step)
+        lax.fori_loop(0, 8, one, 0, unroll=4)
+
+    def send_z(unit):
+        chunk, c = unit // 3, lax.rem(unit, 3)
+        pltpu.make_async_copy(sent1.at[chunk, c, at_y], got1.at[chunk, c, at_y], recv1.at[chunk, c]).start()
+        for step in range(1, 4):
+            to = lax.rem(at_y + step, 4)
             pltpu.make_async_remote_copy(
-                src_ref=sent1.at[chunk, to], dst_ref=got1.at[chunk, gz],
-                send_sem=send1.at[chunk], recv_sem=recv1.at[chunk],
-                device_id=(gy, to), device_id_type=MESH,
+                src_ref=sent1.at[chunk, c, to], dst_ref=got1.at[chunk, c, at_y],
+                send_sem=send1.at[chunk, c], recv_sem=recv1.at[chunk, c],
+                device_id=(gy, at_lo * 4 + to), device_id_type=MESH,
             ).start()
-            return carry
-
-        lax.fori_loop(1, 8, one, 0)
 
     transform_z(0)
-    pl.semaphore_wait(barrier, 38)
-
-    def stage_z(chunk, carry):
-        send_z(chunk)
-
-        @pl.when(chunk < J - 1)
-        def _():
-            transform_z(chunk + 1)
+    pl.semaphore_wait(barrier, 66)
+
+    def stage_z(unit, carry):
+        send_z(unit)
+
+        @pl.when(unit < 3 * J - 1)
+        def _():
+            transform_z(unit + 1)
 
         return carry
 
-    lax.fori_loop(0, J, stage_z, 0)
+    lax.fori_loop(0, 3 * J, stage_z, 0)
     loads[2].wait()
     loads[3].wait()
-
-    def stage_y(chunk, carry):
-        pltpu.make_async_copy(got1.at[chunk], got1.at[chunk], recv1.at[chunk]).wait()
-
-        def one(c, inner):
-            rows = jnp.concatenate(
-                [got1[chunk, s, pl.ds(c * 8, 8)].reshape(128, 128) for s in range(8)], axis=1
-            )
-            for half in range(2):
+    loads[4].wait()
+    ty[...] = raw_y[...].astype(BF)
+    take[...] = raw_take[...].astype(BF)
+    tx[...] = raw_x[...].astype(BF)
+
+    def rows_of(chunk, c):
+        return jnp.concatenate([got1[chunk, c, s].reshape(256, 128) for s in range(4)], axis=1)
+
+    def half_copy(chunk, c):
+        return pltpu.make_async_remote_copy(
+            src_ref=half_out.at[chunk, c], dst_ref=half_in.at[chunk, c],
+            send_sem=sendh.at[chunk, c], recv_sem=recvh.at[chunk, c],
+            device_id=(gy, twin), device_id_type=MESH,
+        )
+
+    def push_y(chunk):
+        def push(step, carry):
+            to_x = lax.rem(at_x + step // 8, 4)
+            place = lax.rem(step // 4 + at_hi, 2)
+            to_hi = jnp.where(half == 0, 3 * place, 1 + place)
+            to_lo = lax.rem(step // 2 + at_lo, 2)
+            to_core = lax.rem(step + at_core, 2)
+            slot = (to_x * 4 + place * 2 + to_core) * 2 + to_lo
+            to = to_x * 8 + to_hi * 2 + to_core
+            same = jnp.logical_and(to == gy, to_lo == at_lo)
+
+            @pl.when(same)
+            def _():
+                pltpu.make_async_copy(sent2.at[chunk, slot], got2.at[chunk, gy], recv2.at[chunk]).start()
+
+            @pl.when(jnp.logical_not(same))
+            def _():
+                pltpu.make_async_remote_copy(
+                    src_ref=sent2.at[chunk, slot], dst_ref=got2.at[chunk, gy],
+                    send_sem=send2.at[chunk], recv_sem=recv2.at[chunk],
+                    device_id=(to, to_lo * 4 + at_y), device_id_type=MESH,
+                ).start()
+
+            return carry
+
+        lax.fori_loop(0, 32, push, 0)
+
+    def stage_y(unit, carry):
+        @pl.when(unit < 3 * J)
+        def _():
+            chunk, c = unit // 3, lax.rem(unit, 3)
+            pltpu.make_async_copy(got1.at[chunk, c], got1.at[chunk, c], recv1.at[chunk, c]).wait()
+            half_out[chunk, c] = lax.dot_general(
+                ty[512:, :], rows_of(chunk, c), (((1,), (1,)), ((), ())), preferred_element_type=F32
+            ).astype(BF)
+            half_copy(chunk, c).start()
+
+        @pl.when(unit >= 1)
+        def _():
+            chunk, c = (unit - 1) // 3, lax.rem(unit - 1, 3)
+            half_copy(chunk, c).wait_recv()
+            rows = rows_of(chunk, c)
+            theirs = half_in[chunk, c]
+            for parity in range(2):
                 out = lax.dot_general(
-                    ty[half * N : (half + 1) * N, :], rows, (((1,), (1,)), ((), ())), preferred_element_type=F32
-                ).astype(BF)
-                for g in range(32):
-                    sent2[chunk, g, c, half] = out[g * 16 : (g + 1) * 16]
-            return inner
-
-        lax.fori_loop(0, 3, one, 0)
-        pltpu.make_async_copy(sent2.at[chunk, gy], got2.at[chunk, gy], recv2.at[chunk]).start()
-
-        def push(step, inner):
-            to = gy_at(step)
-            pltpu.make_async_remote_copy(
-                src_ref=sent2.at[chunk, to], dst_ref=got2.at[chunk, gy],
-                send_sem=send2.at[chunk], recv_sem=recv2.at[chunk],
-                device_id=(to, gz), device_id_type=MESH,
-            ).start()
-            return inner
-
-        lax.fori_loop(1, 32, push, 0)
+                    ty[parity * 256 : parity * 256 + 256, :], rows, (((1,), (1,)), ((), ())), preferred_element_type=F32
+                )
+                out = out + jnp.dot(
+                    take[parity * 256 : parity * 256 + 256, :], theirs, preferred_element_type=F32
+                )
+                out = out.astype(BF)
+                for d in range(16):
+                    for lo in range(2):
+                        sent2[chunk, d * 2 + lo, c, parity] = out[d * 16 : d * 16 + 16, lo * 128 : lo * 128 + 128]
+
+            @pl.when(c == 2)
+            def _():
+                push_y(chunk)
+
         return carry
 
-    lax.fori_loop(0, J, stage_y, 0)
+    lax.fori_loop(0, 3 * J + 1, stage_y, 0)
 
     lane = lax.broadcasted_iota(jnp.int32, (16, 128), 1)
 
@@ -255,35 +357,51 @@
     lax.fori_loop(0, 2, combine, 0)
 
     for chunk in range(J):
-        first = sent1.at[chunk, pl.ds(0, 7)]
-        pltpu.make_async_copy(first, first, send1.at[chunk]).wait()
-        second = sent2.at[chunk, pl.ds(0, 31)]
-        pltpu.make_async_copy(second, second, send2.at[chunk]).wait()
         for c in range(3):
+            first = sent1.at[chunk, c, pl.ds(0, 3)]
+            pltpu.make_async_copy(first, first, send1.at[chunk, c]).wait()
+            half_copy(chunk, c).wait_send()
             pltpu.make_async_copy(field.at[chunk, c], field.at[chunk, c], store_sem.at[chunk, c]).wait()
+
+        @pl.when(in_half)
+        def _():
+            second = sent2.at[chunk, pl.ds(0, 31)]
+            pltpu.make_async_copy(second, second, send2.at[chunk]).wait()
+
+        @pl.when(jnp.logical_not(in_half))
+        def _():
+            pltpu.make_async_copy(sent2.at[chunk], sent2.at[chunk], send2.at[chunk]).wait()
+
     for pair in range(2):
         third = pic_out.at[pair, pl.ds(0, 31)]
         pltpu.make_async_copy(third, third, send3.at[pair]).wait()
 
 
 def shards(coeffs):
-    table_z, table_y, table_x = (jnp.asarray(table) for table in tables())
+    table_z, table_y, table_take, table_x = (jnp.asarray(table) for table in tables())
     any_space = pl.BlockSpec(memory_space=pl.ANY)
     current, bricks = pl.pallas_call(
         kernel,
         out_shape=(
-            jax.ShapeDtypeStruct((3, 16, 64, N), F32),
+            pltpu.VMEM((3, 16, 64, N), F32),
             jax.ShapeDtypeStruct((2, 16, 128), F32),
         ),
-        in_specs=[any_space] * 4,
-        out_specs=(any_space, pl.BlockSpec(memory_space=pltpu.VMEM)),
+        in_specs=[any_space] * 5,
+        out_specs=(pl.BlockSpec(memory_space=pltpu.VMEM), pl.BlockSpec(memory_space=pltpu.VMEM)),
         scratch_shapes=[
+            pltpu.VMEM((N, N), F32),
+            pltpu.VMEM((512 + 2 * SLOTS, N), F32),
+            pltpu.VMEM((512, 2 * SLOTS), F32),
+            pltpu.VMEM((N, N), F32),
             pltpu.VMEM((24, 128, N), BF),
             pltpu.VMEM((N, N), BF),
-            pltpu.VMEM((2 * N, 2 * N), BF),
+            pltpu.VMEM((512 + 2 * SLOTS, N), BF),
+            pltpu.VMEM((512, 2 * SLOTS), BF),
             pltpu.VMEM((N, N), BF),
-            pltpu.VMEM((J, 8, 24, ZC, 128), BF),
-            pltpu.VMEM((J, 8, 24, ZC, 128), BF),
+            pltpu.VMEM((J, 3, 4, 2, 8, ZC, 128), BF),
+            pltpu.VMEM((J, 3, 4, 2, 8, ZC, 128), BF),
+            pltpu.VMEM((J, 3, 2 * SLOTS, 256), BF),
+            pltpu.VMEM((J, 3, 2 * SLOTS, 256), BF),
             pltpu.VMEM((J, 32, 3, 2, 16, 128), BF),
             pltpu.VMEM((J, 32, 3, 2, 16, 128), BF),
             pltpu.VMEM((256, N), BF),
@@ -291,9 +409,11 @@
             pltpu.VMEM((128, N), F32),
             pltpu.VMEM((2, 32, 16, 128), BF),
             pltpu.VMEM((2, 32, 16, 128), BF),
-            pltpu.SemaphoreType.DMA((4,)),
-            pltpu.SemaphoreType.DMA((J,)),
-            pltpu.SemaphoreType.DMA((J,)),
+            pltpu.SemaphoreType.DMA((5,)),
+            pltpu.SemaphoreType.DMA((J, 3)),
+            pltpu.SemaphoreType.DMA((J, 3)),
+            pltpu.SemaphoreType.DMA((J, 3)),
+            pltpu.SemaphoreType.DMA((J, 3)),
             pltpu.SemaphoreType.DMA((J,)),
             pltpu.SemaphoreType.DMA((J,)),
             pltpu.SemaphoreType.DMA((2,)),
@@ -304,7 +424,12 @@
             collective_id=0, has_side_effects=True, vmem_limit_bytes=48 * 1024 * 1024
         ),
         name="render",
-    )(coeffs.reshape(24, 128, N), table_z, table_y, table_x)
+    )(
+        *(
+            pltpu.with_memory_space_constraint(operand, pltpu.HBM)
+            for operand in (coeffs.reshape(24, 128, N), table_z, table_y, table_take, table_x)
+        )
+    )
     picture = bricks.reshape(2, 16, 2, 4, ZC).transpose(3, 0, 2, 4, 1).reshape(4, 64, 16)
     return (current, picture)
 

time: 143 us -> 135 us (0.944)
  local copies, waits for them, and re-layouts: 11.4 us -> 3.68 us
    unnamed x7 -> x3, local copies, waits for them, and re-layouts: 10.4 us -> 2.71 us
where the time goes in v2:
time: 135 us
  Pallas kernels  131 us (97%)
  local copies, waits for them, and re-layouts  3.68 us (3%)
    pallas_call x1, Pallas kernels, shards(): pl.pallas_call(kernel, out_shape=(pltpu.VMEM((3, 16, 64, N), F32), jax.Sh...  131 us
    unnamed x3, local copies, waits for them, and re-layouts  2.71 us

profile of v2, /device:TPU:1, one launch (start us, length us, event | category | flops | bytes accessed | tf_op | source)
XLA Modules:
  0.0 135.1 jit_solution(1808466142023710)
XLA Ops:
  0.6 130.7 %render.1 = (f32[3,16,64,512]{3,2,1,0:T(8,128)S(1)}, f32[2,16,128]{2,1,0:T(8,128)}) custom-call(bf16[24,128,512]{2,1,0:T(8,128)(2,1)} %bitcast.4, f32[512,512]{1,0:T(8,128)} %constant.8.clone.tz_hbm, f32[4,784,512]{2,1,0:T(8,128)} %constant.9.clone.ty_hbm, f32[4,512,272]{2,1,0:T(8,128)} %constant.10.clone.take_hbm, f32[512,512]{1,0:T(8,128)} %constant.11.clone.tx_hbm), custom_call_target="tpu_custom_call" | custom-call | tf_op jit(solution)/shard_map/render/pallas_call | solution.py:383
  131.4 0.0 copy-start
  131.4 2.7 %copy.9 = f32[3,16,64,512]{3,2,1,0:T(8,128)} copy(f32[3,16,64,512]{3,2,1,0:T(8,128)S(1)} %get-tuple-element.6) | data formatting | bytes 12582912
  134.1 0.0 copy-done
  134.1 0.1 reshape.14
  134.2 0.1 copy.7
  134.3 0.8 reshape.15
Async XLA Ops:
  131.4 2.7 %copy-start = (f32[2,16,128]{2,1,0:T(8,128)S(1)}, f32[2,16,128]{2,1,0:T(8,128)}, u32[]{:S(2)}) copy-start(f32[2,16,128]{2,1,0:T(8,128)} %get-tuple-element.5) | copy-start | bytes 49156

commit v3 on v2

--- a/solution.py
+++ b/solution.py
@@ -13,6 +13,7 @@
 N = 512
 J = 4
 ZC = 16
+AHEAD = 2
 MESH = pl.DeviceIdType.MESH
 BF, F32 = jnp.bfloat16, jnp.float32
 
@@ -90,10 +91,10 @@
 
 
 def kernel(
-    coef_hbm, tz_hbm, ty_hbm, take_hbm, tx_hbm, current_hbm, bricks_ref,
+    coef_hbm, tz_hbm, ty_hbm, take_hbm, tx_hbm, current_ref, picture_ref,
     raw_z, raw_y, raw_take, raw_x,
-    coef, tz, ty, take, tx, sent1, got1, half_out, half_in, sent2, got2, rows_x, field, tint, pic_out, pic_in,
-    load_sem, send1, recv1, sendh, recvh, send2, recv2, send3, recv3, store_sem,
+    coef, tz, ty, take, tx, sent1, got1, half_out, half_in, sent2, got2, rows_x, field, tint, done, pic_half, pic_near, pic_out, pic_in,
+    load_sem, send1, recv1, sendh, recvh, send2, recv2, sendb, recvb, send3, recv3, store_sem,
 ):
     gy, gz = lax.axis_index("gy"), lax.axis_index("gz")
     at_x, at_hi, at_core = gy // 8, lax.rem(gy // 2, 4), lax.rem(gy, 2)
@@ -123,17 +124,20 @@
 
     loads = [
         pltpu.make_async_copy(tz_hbm, raw_z, load_sem.at[0]),
-        pltpu.make_async_copy(coef_hbm, coef, load_sem.at[1]),
+        pltpu.make_async_copy(coef_hbm.at[pl.ds(0, 8)], coef.at[pl.ds(0, 8)], load_sem.at[1]),
+        pltpu.make_async_copy(coef_hbm.at[pl.ds(8, 16)], coef.at[pl.ds(8, 16)], load_sem.at[5]),
         pltpu.make_async_copy(ty_hbm.at[kind], raw_y, load_sem.at[2]),
         pltpu.make_async_copy(take_hbm.at[kind], raw_take, load_sem.at[3]),
         pltpu.make_async_copy(tx_hbm, raw_x, load_sem.at[4]),
     ]
-    for load in loads:
-        load.start()
+    loads[0].start()
+    loads[1].start()
     for step in range(1, 4):
         pl.semaphore_signal(barrier, inc=1, device_id=(gy, y_at(step)), device_id_type=MESH)
     pl.semaphore_signal(barrier, inc=1, device_id=(gy, twin), device_id_type=MESH)
     lax.fori_loop(1, 32, greet, 0)
+    for load in loads[2:]:
+        load.start()
     loads[0].wait()
     tz[...] = raw_z[...].astype(BF)
     loads[1].wait()
@@ -167,20 +171,14 @@
 
     transform_z(0)
     pl.semaphore_wait(barrier, 66)
-
-    def stage_z(unit, carry):
+    send_z(0)
+    loads[2].wait()
+    for unit in range(1, AHEAD):
+        transform_z(unit)
         send_z(unit)
-
-        @pl.when(unit < 3 * J - 1)
-        def _():
-            transform_z(unit + 1)
-
-        return carry
-
-    lax.fori_loop(0, 3 * J, stage_z, 0)
-    loads[2].wait()
     loads[3].wait()
     loads[4].wait()
+    loads[5].wait()
     ty[...] = raw_y[...].astype(BF)
     take[...] = raw_take[...].astype(BF)
     tx[...] = raw_x[...].astype(BF)
@@ -205,15 +203,16 @@
             slot = (to_x * 4 + place * 2 + to_core) * 2 + to_lo
             to = to_x * 8 + to_hi * 2 + to_core
             same = jnp.logical_and(to == gy, to_lo == at_lo)
+            source, target = sent2.at[chunk, slot], got2.at[chunk, gy]
 
             @pl.when(same)
             def _():
-                pltpu.make_async_copy(sent2.at[chunk, slot], got2.at[chunk, gy], recv2.at[chunk]).start()
+                pltpu.make_async_copy(source, target, recv2.at[chunk]).start()
 
             @pl.when(jnp.logical_not(same))
             def _():
                 pltpu.make_async_remote_copy(
-                    src_ref=sent2.at[chunk, slot], dst_ref=got2.at[chunk, gy],
+                    src_ref=source, dst_ref=target,
                     send_sem=send2.at[chunk], recv_sem=recv2.at[chunk],
                     device_id=(to, to_lo * 4 + at_y), device_id_type=MESH,
                 ).start()
@@ -231,6 +230,11 @@
                 ty[512:, :], rows_of(chunk, c), (((1,), (1,)), ((), ())), preferred_element_type=F32
             ).astype(BF)
             half_copy(chunk, c).start()
+
+        @pl.when(unit + AHEAD < 3 * J)
+        def _():
+            transform_z(unit + AHEAD)
+            send_z(unit + AHEAD)
 
         @pl.when(unit >= 1)
         def _():
@@ -260,7 +264,65 @@
 
     lane = lax.broadcasted_iota(jnp.int32, (16, 128), 1)
 
+    channel = (lane // ZC) % 4
+    is_depth = channel == 3
+
+    sibling = gy + 1 - 2 * at_core
+
+    def sibling_copy(pair):
+        return pltpu.make_async_remote_copy(
+            src_ref=pic_half.at[pair, 1 - at_core], dst_ref=pic_near.at[pair],
+            send_sem=sendb.at[pair], recv_sem=recvb.at[pair],
+            device_id=(sibling, gz), device_id_type=MESH,
+        )
+
+    def spread_depth(brick):
+        depth = jnp.where(is_depth, brick, 0.0)
+        depth = depth + pltpu.roll(depth, 128 - 16, 1)
+        return depth + pltpu.roll(depth, 128 - 32, 1)
+
+    def send_pair(pair):
+        sibling_copy(pair).wait_recv()
+        for m in range(16):
+            mine = pic_half[pair, at_core, m].astype(F32)
+            theirs = pic_near[pair, m].astype(F32)
+            front = jnp.where(at_core == 0, mine, theirs)
+            back = jnp.where(at_core == 0, theirs, mine)
+            passed = jnp.where(is_depth, 1.0, jnp.exp(-spread_depth(front)))
+            pic_out[pair, m] = (front + passed * back).astype(BF)
+        here = gy // 2
+        pltpu.make_async_copy(pic_out.at[pair, here], pic_in.at[pair, here], recv3.at[pair]).start()
+
+        def push(step, inner):
+            to = lax.rem(here // 4 + step // 4, 4) * 4 + lax.rem(here + step, 4)
+            pltpu.make_async_remote_copy(
+                src_ref=pic_out.at[pair, to], dst_ref=pic_in.at[pair, here],
+                send_sem=send3.at[pair], recv_sem=recv3.at[pair],
+                device_id=(to * 2 + at_core, gz), device_id_type=MESH,
+            ).start()
+            return inner
+
+        lax.fori_loop(1, 16, push, 0)
+
+    def combine(pair):
+        pltpu.make_async_copy(pic_in.at[pair], pic_in.at[pair], recv3.at[pair]).wait()
+        before = jnp.zeros((16, 128), F32)
+        total = jnp.zeros((16, 128), F32)
+        for m in range(16):
+            brick = pic_in[pair, m].astype(F32)
+            total = total + jnp.exp(-before) * brick
+            before = before + spread_depth(brick)
+        done[pl.ds(pair * 16, 16), :] = jnp.where(is_depth, 1.0 - jnp.exp(-before), total)
+
     def stage_x(chunk, carry):
+        @pl.when(chunk == 2)
+        def _():
+            send_pair(0)
+
+        @pl.when(chunk == J - 1)
+        def _():
+            combine(0)
+
         pltpu.make_async_copy(got2.at[chunk], got2.at[chunk], recv2.at[chunk]).wait()
 
         def component(c, inner):
@@ -283,7 +345,7 @@
                     ]
                 pltpu.make_async_copy(
                     field.at[chunk, c, col].reshape(16, ZC, 128),
-                    current_hbm.at[c, :, pl.ds(chunk * ZC, ZC), pl.ds(col * 128, 128)],
+                    current_ref.at[c, :, pl.ds(chunk * ZC, ZC), pl.ds(col * 128, 128)],
                     store_sem.at[chunk, c],
                 ).start()
             return inner
@@ -319,42 +381,20 @@
             for col in range(4):
                 turned = jnp.transpose(tint[:, col * 128 : (col + 1) * 128]).astype(BF)
                 for g in range(8):
-                    pic_out[pair, col * 8 + g] = turned[g * 16 : (g + 1) * 16]
-            pltpu.make_async_copy(pic_out.at[pair, gy], pic_in.at[pair, gy], recv3.at[pair]).start()
-
-            def push(step, inner):
-                to = gy_at(step)
-                pltpu.make_async_remote_copy(
-                    src_ref=pic_out.at[pair, to], dst_ref=pic_in.at[pair, gy],
-                    send_sem=send3.at[pair], recv_sem=recv3.at[pair],
-                    device_id=(to, gz), device_id_type=MESH,
-                ).start()
-                return inner
-
-            lax.fori_loop(1, 32, push, 0)
+                    pic_half[pair, g % 2, col * 4 + g // 2] = turned[g * 16 : (g + 1) * 16]
+            sibling_copy(pair).start()
 
         return carry
 
     lax.fori_loop(0, J, stage_x, 0)
 
-    channel = (lane // ZC) % 4
-    is_depth = channel == 3
-
-    def combine(pair, carry):
-        pltpu.make_async_copy(pic_in.at[pair], pic_in.at[pair], recv3.at[pair]).wait()
-        before = jnp.zeros((16, 128), F32)
-        total = jnp.zeros((16, 128), F32)
-        for s in range(32):
-            brick = pic_in[pair, s].astype(F32)
-            depth = jnp.where(is_depth, brick, 0.0)
-            depth = depth + pltpu.roll(depth, 128 - 16, 1)
-            depth = depth + pltpu.roll(depth, 128 - 32, 1)
-            total = total + jnp.exp(-before) * brick
-            before = before + depth
-        bricks_ref[pair] = jnp.where(is_depth, 1.0 - jnp.exp(-before), total)
-        return carry
-
-    lax.fori_loop(0, 2, combine, 0)
+    send_pair(1)
+    combine(1)
+    for pair in range(2):
+        for part in range(2):
+            for k in range(4):
+                start, place = (part * 4 + k) * ZC, (pair * 2 + part) * ZC
+                picture_ref[k, :, place : place + ZC] = done[pair * 16 : pair * 16 + 16, start : start + ZC]
 
     for chunk in range(J):
         for c in range(3):
@@ -373,18 +413,19 @@
             pltpu.make_async_copy(sent2.at[chunk], sent2.at[chunk], send2.at[chunk]).wait()
 
     for pair in range(2):
-        third = pic_out.at[pair, pl.ds(0, 31)]
+        sibling_copy(pair).wait_send()
+        third = pic_out.at[pair, pl.ds(0, 15)]
         pltpu.make_async_copy(third, third, send3.at[pair]).wait()
 
 
 def shards(coeffs):
     table_z, table_y, table_take, table_x = (jnp.asarray(table) for table in tables())
     any_space = pl.BlockSpec(memory_space=pl.ANY)
-    current, bricks = pl.pallas_call(
+    current, picture = pl.pallas_call(
         kernel,
         out_shape=(
             pltpu.VMEM((3, 16, 64, N), F32),
-            jax.ShapeDtypeStruct((2, 16, 128), F32),
+            pltpu.VMEM((4, 16, 64), F32),
         ),
         in_specs=[any_space] * 5,
         out_specs=(pl.BlockSpec(memory_space=pltpu.VMEM), pl.BlockSpec(memory_space=pltpu.VMEM)),
@@ -407,15 +448,20 @@
             pltpu.VMEM((256, N), BF),
             pltpu.VMEM((J, 3, 4, 16 * ZC, 128), F32),
             pltpu.VMEM((128, N), F32),
-            pltpu.VMEM((2, 32, 16, 128), BF),
-            pltpu.VMEM((2, 32, 16, 128), BF),
-            pltpu.SemaphoreType.DMA((5,)),
+            pltpu.VMEM((32, 128), F32),
+            pltpu.VMEM((2, 2, 16, 16, 128), BF),
+            pltpu.VMEM((2, 16, 16, 128), BF),
+            pltpu.VMEM((2, 16, 16, 128), BF),
+            pltpu.VMEM((2, 16, 16, 128), BF),
+            pltpu.SemaphoreType.DMA((6,)),
             pltpu.SemaphoreType.DMA((J, 3)),
             pltpu.SemaphoreType.DMA((J, 3)),
             pltpu.SemaphoreType.DMA((J, 3)),
             pltpu.SemaphoreType.DMA((J, 3)),
             pltpu.SemaphoreType.DMA((J,)),
             pltpu.SemaphoreType.DMA((J,)),
+            pltpu.SemaphoreType.DMA((2,)),
+            pltpu.SemaphoreType.DMA((2,)),
             pltpu.SemaphoreType.DMA((2,)),
             pltpu.SemaphoreType.DMA((2,)),
             pltpu.SemaphoreType.DMA((J, 3)),
@@ -430,8 +476,7 @@
             for operand in (coeffs.reshape(24, 128, N), table_z, table_y, table_take, table_x)
         )
     )
-    picture = bricks.reshape(2, 16, 2, 4, ZC).transpose(3, 0, 2, 4, 1).reshape(4, 64, 16)
-    return (current, picture)
+    return (current, picture.transpose(0, 2, 1))
 
 
 def solution(mesh):

time: 135 us -> 131 us (0.970)
  Pallas kernels: 131 us -> 127 us
    pallas_call x1, Pallas kernels: 131 us -> 127 us  [shards(): pl.pallas_call(kernel, out_shape=(pltpu.VMEM((3, 16, 64, N), F32), pltpu....]
    unnamed x3 -> x2, local copies, waits for them, and re-layouts: 2.71 us -> 3.32 us
where the time goes in v3:
time: 131 us
  Pallas kernels  127 us (97%)
  local copies, waits for them, and re-layouts  3.32 us (3%)
    pallas_call x1, Pallas kernels, shards(): pl.pallas_call(kernel, out_shape=(pltpu.VMEM((3, 16, 64, N), F32), pltpu....  127 us
    unnamed x2, local copies, waits for them, and re-layouts  3.32 us

profile of v3, /device:TPU:1, one launch (start us, length us, event | category | flops | bytes accessed | tf_op | source)
XLA Modules:
  0.0 130.6 jit_solution(577639008078078188)
XLA Ops:
  0.6 126.7 %render.1 = (f32[3,16,64,512]{3,2,1,0:T(8,128)S(1)}, f32[4,16,64]{2,1,0:T(8,128)S(1)}) custom-call(bf16[24,128,512]{2,1,0:T(8,128)(2,1)} %bitcast.3, f32[512,512]{1,0:T(8,128)} %constant.8.clone.tz_hbm, f32[4,784,512]{2,1,0:T(8,128)} %constant.9.clone.ty_hbm, f32[4,512,272]{2,1,0:T(8,128)} %constant.10.clone.take_hbm, f32[512,512]{1,0:T(8,128)} %constant.11.clone.tx_hbm), custom_call_target="tpu_custom_call" | custom-call | tf_op jit(solution)/shard_map/render/pallas_call | solution.py:424
  127.3 2.7 %copy.9 = f32[3,16,64,512]{3,2,1,0:T(8,128)} copy(f32[3,16,64,512]{3,2,1,0:T(8,128)S(1)} %get-tuple-element.6) | data formatting | bytes 12582912
  130.0 0.6 copy.10

commit v4 on v3

--- a/solution.py
+++ b/solution.py
@@ -193,7 +193,7 @@
             device_id=(gy, twin), device_id_type=MESH,
         )
 
-    def push_y(chunk):
+    def push_y(chunk, first, count):
         def push(step, carry):
             to_x = lax.rem(at_x + step // 8, 4)
             place = lax.rem(step // 4 + at_hi, 2)
@@ -203,7 +203,8 @@
             slot = (to_x * 4 + place * 2 + to_core) * 2 + to_lo
             to = to_x * 8 + to_hi * 2 + to_core
             same = jnp.logical_and(to == gy, to_lo == at_lo)
-            source, target = sent2.at[chunk, slot], got2.at[chunk, gy]
+            picked = pl.ds(first, count)
+            source, target = sent2.at[chunk, slot, picked], got2.at[chunk, gy, picked]
 
             @pl.when(same)
             def _():
@@ -254,9 +255,17 @@
                     for lo in range(2):
                         sent2[chunk, d * 2 + lo, c, parity] = out[d * 16 : d * 16 + 16, lo * 128 : lo * 128 + 128]
 
-            @pl.when(c == 2)
+            @pl.when(jnp.logical_and(chunk == J - 1, c == 1))
             def _():
-                push_y(chunk)
+                push_y(chunk, 0, 2)
+
+            @pl.when(jnp.logical_and(chunk == J - 1, c == 2))
+            def _():
+                push_y(chunk, 2, 1)
+
+            @pl.when(jnp.logical_and(chunk < J - 1, c == 2))
+            def _():
+                push_y(chunk, 0, 3)
 
         return carry
 
@@ -327,7 +336,7 @@
 
         def component(c, inner):
             for group in range(4):
-                tiles = [got2[chunk, group * 8 + t // 2, c, t % 2].astype(F32) for t in range(16)]
+                tiles = [got2[chunk, group * 8 + t // 2, c, t % 2] for t in range(16)]
                 for bit in (1, 2, 4, 8):
                     low = (lane & bit) == 0
                     for t in range(16):
@@ -336,7 +345,7 @@
                             tiles[t] = jnp.where(low, u, pltpu.roll(v, bit, 1))
                             tiles[t + bit] = jnp.where(low, pltpu.roll(u, 128 - bit, 1), v)
                 for t in range(16):
-                    rows_x[pl.ds(t * 16, 16), pl.ds(group * 128, 128)] = tiles[t].astype(BF)
+                    rows_x[pl.ds(t * 16, 16), pl.ds(group * 128, 128)] = tiles[t]
             out = jnp.dot(rows_x[...], tx[...], preferred_element_type=F32)
             for col in range(4):
                 for t in range(16):
@@ -416,6 +425,20 @@
         sibling_copy(pair).wait_send()
         third = pic_out.at[pair, pl.ds(0, 15)]
         pltpu.make_async_copy(third, third, send3.at[pair]).wait()
+
+
+def write_out(current_ref, picture_ref, current_hbm, picture_hbm, sems):
+    copies = [pltpu.make_async_copy(picture_ref, picture_hbm, sems.at[12])]
+    for c in range(3):
+        for part in range(4):
+            rows = pl.ds(part * 4, 4)
+            copies.append(
+                pltpu.make_async_copy(current_ref.at[c, rows], current_hbm.at[c, rows], sems.at[c * 4 + part])
+            )
+    for copy in copies:
+        copy.start()
+    for copy in copies:
+        copy.wait()
 
 
 def shards(coeffs):
@@ -476,6 +499,15 @@
             for operand in (coeffs.reshape(24, 128, N), table_z, table_y, table_take, table_x)
         )
     )
+    current, picture = pl.pallas_call(
+        write_out,
+        out_shape=(pltpu.HBM((3, 16, 64, N), F32), pltpu.HBM((4, 16, 64), F32)),
+        in_specs=[any_space, any_space],
+        out_specs=(any_space, any_space),
+        scratch_shapes=[pltpu.SemaphoreType.DMA((13,))],
+        compiler_params=pltpu.CompilerParams(vmem_limit_bytes=4 * 1024 * 1024),
+        name="write_out",
+    )(*(pltpu.with_memory_space_constraint(operand, pltpu.VMEM) for operand in (current, picture)))
     return (current, picture.transpose(0, 2, 1))
 
 

time: 131 us -> 130 us (level)
  local copies, waits for them, and re-layouts: 3.32 us -> 0 us
  Pallas kernels: 127 us -> 129 us
    unnamed x2 -> x0, local copies, waits for them, and re-layouts: 3.32 us -> none
    pallas_call x0 -> x1, Pallas kernels: none -> 2.77 us  [shards(): pl.pallas_call(write_out, out_shape=(pltpu.HBM((3, 16, 64, N), F32), pltp...]
where the time goes in v4:
time: 130 us
  Pallas kernels  129 us (99%)
    pallas_call x1, Pallas kernels, shards(): pl.pallas_call(kernel, out_shape=(pltpu.VMEM((3, 16, 64, N), F32), pltpu....  126 us
    pallas_call x1, Pallas kernels, shards(): pl.pallas_call(write_out, out_shape=(pltpu.HBM((3, 16, 64, N), F32), pltp...  2.77 us

profile of v4, /device:TPU:1, one launch (start us, length us, event | category | flops | bytes accessed | tf_op | source)
XLA Modules:
  0.0 129.6 jit_solution(8795961098981168139)
XLA Ops:
  0.6 126.2 %render.1 = (f32[3,16,64,512]{3,2,1,0:T(8,128)S(1)}, f32[4,16,64]{2,1,0:T(8,128)S(1)}) custom-call(bf16[24,128,512]{2,1,0:T(8,128)(2,1)} %bitcast.2, f32[512,512]{1,0:T(8,128)} %constant.8.clone.tz_hbm, f32[4,784,512]{2,1,0:T(8,128)} %constant.9.clone.ty_hbm, f32[4,512,272]{2,1,0:T(8,128)} %constant.10.clone.take_hbm, f32[512,512]{1,0:T(8,128)} %constant.11.clone.tx_hbm), custom_call_target="tpu_custom_call" | custom-call | tf_op jit(solution)/shard_map/render/pallas_call | solution.py:447
  126.8 2.8 %write_out.1 = (f32[3,16,64,512]{3,2,1,0:T(8,128)}, f32[4,16,64]{2,1,0:T(8,128)}) custom-call(f32[3,16,64,512]{3,2,1,0:T(8,128)S(1)} %get-tuple-element.6.current_ref, f32[4,16,64]{2,1,0:T(8,128)S(1)} %get-tuple-element.7.picture_ref), custom_call_target="tpu_custom_call" | custom-call | tf_op jit(solution)/shard_map/write_out/pallas_call | solution.py:502
